TPU v7x, 512 devices: a whole 4x4x16 slice. The times are simulated.
512 devices in a mesh: group: 32 (over z, core), tensor: 16 (over y, x).
Axes of the slice: x: 4, y: 4, z: 16, core: 2. Of those that a mesh axis runs over, the one named last changes fastest.
Arguments:
- queries: bfloat16 [384, 4, 8192], P('group', None, 'tensor'), may hold values from -603 to 603
- new_entries: bfloat16 [384, 4, 2048], P('group'), may hold values from -6 to 6
- resident_cache: bfloat16 [128, 512, 2048], P('group', 'tensor'), may hold values from -6 to 6
- prefill_cache: bfloat16 [256, 512, 2048], P('group', 'tensor'), may hold values from -6 to 6
- resident_kept: int32 [128], replicated, may hold values from 256 to 512, as said below
- kept_tokens: int32 [256], replicated, may hold values from 1 to 512, as said below
- prefill_slot: int32 [256], replicated, may hold values from 0 to 255, as said below
- decode_slot: int32 [256], replicated, may hold values from 4 to 383, as said below
Outputs:
- attended: bfloat16 [384, 4, 8192], P('group', None, 'tensor')
Inputs may be any that keep to these rules, and one draw needn't show every extreme that they name: `kept_tokens`: some request keeps exactly 512 positions. `prefill_slot`: A permutation of the 256 prefill slots; slot s lies in prefill group s // 8. `decode_slot`: every slot g * 12 + l with l >= 4 is named by exactly one request; from one prefill group to one decode group go at most 1 request, and exactly 1 for some pairs. `resident_kept`: some resident request keeps exactly 512 positions.
All inputs are finite; a program needn't handle non-finite values.
Results may differ from a plain program's by a relative error of at most 0.0044.
Values may be sent and summed in bfloat16 or wider, within the bound.
No kernel may reach another device: no remote copies, remote signals or barrier semaphores. Data moves between devices by JAX's collectives and lax.ppermute only.
A program may use at most 128 MiB of HBM per device.

v0:
```python
import math
import jax
import jax.numpy as jnp
from jax import lax
from jax.sharding import PartitionSpec as P

H = 64
KVH = 8
HD = 128
STEPS = 4
MIG_DEV = 8
RES_DEV = 4
NEG_FLOOR = -1e30


def combined_all(part, axis, combine):
    gathered = jax.tree.map(lambda a: lax.all_gather(a, axis), part)

    def take(source):
        return jax.tree.map(lambda a: lax.dynamic_index_in_dim(a, source, 0, False), gathered)

    return lax.fori_loop(
        1, lax.axis_size(axis), lambda source, state: combine(state, take(source)), take(0)
    )


def routing(kept_tokens, prefill_slot, decode_slot, groups, per_pair):
    slot_count = MIG_DEV * groups
    per_group = RES_DEV + MIG_DEV
    dest_by_slot = jnp.zeros((slot_count,), jnp.int32).at[prefill_slot].set(decode_slot)
    kept_by_slot = jnp.zeros((slot_count,), jnp.int32).at[prefill_slot].set(kept_tokens)
    dest_group = (dest_by_slot // per_group).reshape(groups, MIG_DEV)
    earlier = jnp.arange(MIG_DEV)[None, :] < jnp.arange(MIG_DEV)[:, None]
    matching = dest_group[:, :, None] == dest_group[:, None, :]
    ranking = jnp.sum((matching & earlier[None]).astype(jnp.int32), axis=2)
    outgoing_row = (dest_group * per_pair + ranking).reshape(slot_count)
    source_by_dslot = jnp.zeros((groups * per_group,), jnp.int32).at[decode_slot].set(prefill_slot)
    return (kept_by_slot, ranking.reshape(slot_count), outgoing_row, source_by_dslot)


def partials(asking, stored, lengths, offset):
    row_count = stored.shape[0]
    stride = stored.shape[1]
    sharing = H // KVH
    asked_rows = asking.reshape(row_count, STEPS, KVH, sharing, HD)
    entries = stored.reshape(row_count, stride, 2, KVH, HD)
    scores = jnp.einsum(
        "rtkgd,rpkd->rtkgp", asked_rows, entries[:, :, 0], preferred_element_type=jnp.float32
    ) * (1.0 / math.sqrt(HD))
    usable = (offset + jnp.arange(stride))[None, :] < lengths[:, None]
    usable = usable[:, None, None, None, :]
    highest = jnp.max(jnp.where(usable, scores, NEG_FLOOR), axis=4)
    weights = jnp.where(usable, jnp.exp(scores - highest[..., None]), 0.0)
    totals = jnp.sum(weights, axis=4)
    blended = jnp.einsum(
        "rtkgp,rpkd->rtkgd",
        weights.astype(jnp.bfloat16),
        entries[:, :, 1],
        preferred_element_type=jnp.float32,
    )
    return (
        highest.reshape(row_count, STEPS, H),
        totals.reshape(row_count, STEPS, H),
        blended.reshape(row_count, STEPS, H, HD),
    )


def combine(earlier, later):
    highest = jnp.maximum(earlier[0], later[0])
    first_factor = jnp.exp(earlier[0] - highest)
    second_factor = jnp.exp(later[0] - highest)
    return (
        highest,
        earlier[1] * first_factor + later[1] * second_factor,
        earlier[2] * first_factor[..., None] + later[2] * second_factor[..., None],
    )


def own_heads(parts):
    shards = lax.axis_size("tensor")
    stride_heads = H // shards
    merged = combined_all(parts, "tensor", combine)
    start_head = lax.axis_index("tensor") * stride_heads
    result = tuple(
        (lax.dynamic_slice_in_dim(member, start_head, stride_heads, 2) for member in merged)
    )
    return result


def body(
    queries,
    new_entries,
    resident_cache,
    prefill_cache,
    resident_kept,
    kept_tokens,
    prefill_slot,
    decode_slot,
):
    groups = lax.axis_size("group")
    shards = lax.axis_size("tensor")
    per_pair = max(1, MIG_DEV // groups)
    per_group = RES_DEV + MIG_DEV
    stride = prefill_cache.shape[1]
    features = prefill_cache.shape[2]
    offset = lax.axis_index("tensor") * stride
    group_here = lax.axis_index("group")
    kept_by_slot, ranking, outgoing_row, source_by_dslot = routing(
        kept_tokens, prefill_slot, decode_slot, groups, per_pair
    )
    local_rows = lax.dynamic_slice_in_dim(outgoing_row, group_here * MIG_DEV, MIG_DEV)
    arriving = lax.dynamic_slice_in_dim(source_by_dslot, group_here * per_group + RES_DEV, MIG_DEV)
    arriving_rows = arriving // MIG_DEV * per_pair + ranking[arriving]
    arriving_kept = kept_by_slot[arriving]
    resident_len = lax.dynamic_slice_in_dim(resident_kept, group_here * RES_DEV, RES_DEV)
    asking = lax.all_gather(queries, "tensor", axis=2, tiled=True)
    resident_parts = partials(asking[:RES_DEV], resident_cache, resident_len, offset)
    outgoing = (
        jnp.zeros((groups * per_pair, stride, features), jnp.bfloat16)
        .at[local_rows]
        .set(prefill_cache)
    )
    arrived = lax.all_to_all(
        outgoing.reshape(groups, per_pair, stride, features),
        "group",
        split_axis=0,
        concat_axis=0,
        tiled=True,
    )
    moved_cache = arrived.reshape(groups * per_pair, stride, features)[arriving_rows]
    moved_parts = partials(asking[RES_DEV:], moved_cache, arriving_kept, offset)
    heads_parts = own_heads(
        tuple(
            (
                jnp.concatenate([former, latter], 0)
                for former, latter in zip(resident_parts, moved_parts)
            )
        )
    )
    highest, totals, blended = heads_parts
    stride_heads = H // shards
    sharing = H // KVH
    heads_here = lax.axis_index("tensor") * stride_heads + jnp.arange(stride_heads)
    pairs_here = heads_here // sharing
    asked_here = queries.reshape(per_group, STEPS, stride_heads, HD)
    newest = new_entries.reshape(per_group, STEPS, 2, KVH, HD)
    new_keys = jnp.take(newest[:, :, 0], pairs_here, axis=2)
    new_values = jnp.take(newest[:, :, 1], pairs_here, axis=2)
    scores = jnp.einsum(
        "rthd,ruhd->rthu", asked_here, new_keys, preferred_element_type=jnp.float32
    ) * (1.0 / math.sqrt(HD))
    causal = (jnp.arange(STEPS)[None, :] <= jnp.arange(STEPS)[:, None])[None, :, None, :]
    new_high = jnp.max(jnp.where(causal, scores, NEG_FLOOR), axis=3)
    overall = jnp.maximum(highest, new_high)
    weights = jnp.where(causal, jnp.exp(scores - overall[..., None]), 0.0)
    carried = jnp.exp(highest - overall)
    totals = totals * carried + jnp.sum(weights, axis=3)
    blended = blended * carried[..., None] + jnp.einsum(
        "rthu,ruhd->rthd",
        weights.astype(jnp.bfloat16),
        new_values,
        preferred_element_type=jnp.float32,
    )
    return (
        (blended / totals[..., None])
        .astype(jnp.bfloat16)
        .reshape(per_group, STEPS, stride_heads * HD)
    )


def solution(mesh):
    in_specs = (
        P("group", None, "tensor"),
        P("group", None, None),
        P("group", "tensor", None),
        P("group", "tensor", None),
        P(),
        P(),
        P(),
        P(),
    )
    out_specs = P("group", None, "tensor")
    return jax.shard_map(body, mesh=mesh, in_specs=in_specs, out_specs=out_specs, check_vma=False)
```

profile of v0, /device:TPU:1, one launch (start us, length us, event | category | flops | bytes accessed | tf_op | source)
XLA Modules:
  0.0 440.8 jit_solution(7627150290861144147)
XLA Ops:
  6.5 0.7 compare_select_fusion
  7.2 1.6 scatter_custom_fusion.2
  9.3 2.5 broadcast_in_dim.118
  11.8 2.9 scatter_fusion
  14.7 16.9 %all-to-all-start = ((bf16[32,1,32,2048]{3,2,1,0:T(8,128)(2,1)}), bf16[32,1,32,2048]{3,2,1,0:T(8,128)(2,1)}, u32[]{:S(2)}, u32[]{:S(2)}) async-start(bf16[32,1,32,2048]{3,2,1,0:T(8,128)(2,1)} %bitcast.125), calls=%async_computation | async-start | bytes 8388608 | tf_op jit(solution)/shard_map/all_to_all | solution.py:123
  31.7 22.6 %all_gather.21 = bf16[12,4,8192]{2,1,0:T(4,128)(2,1)S(1)} all-gather(bf16[12,4,512]{2,1,0:T(4,128)(2,1)S(1)} %copy-done.4), channel_id=1, replica_groups=mesh['group'=32,'tensor'=16] {'tensor'}, dimensions={2}, use_global_device_ids=true | all-gather | bytes 835584 | tf_op jit(solution)/shard_map/all_gather | solution.py:116
  54.3 0.2 slice.51
  54.6 1.7 scatter_custom_fusion.1
  56.4 0.6 gather_fusion.1
  57.1 1.6 scatter_custom_fusion
  58.6 0.6 gather_fusion
  59.3 0.5 reshape.250
  59.8 0.3 reshape.138
  60.1 0.1 copy.179
  60.5 0.4 select_reduce_fusion.1
  60.9 0.3 convolution_bitcast_fusion.1
  61.5 153.5 %all-to-all-done = bf16[32,1,32,2048]{3,2,1,0:T(8,128)(2,1)} async-done(((bf16[32,1,32,2048]{3,2,1,0:T(8,128)(2,1)}), bf16[32,1,32,2048]{3,2,1,0:T(8,128)(2,1)}, u32[]{:S(2)}, u32[]{:S(2)}) %all-to-all-start) | async-done | bytes 4194336 | tf_op jit(solution)/shard_map/all_to_all | solution.py:123
  214.9 2.8 gather_fusion.2
  217.7 0.2 copy.180
  218.0 0.2 fusion.41
  218.2 0.5 select_reduce_fusion
  218.7 0.7 convolution_bitcast_fusion
  219.4 0.1 copy.209
  219.5 1.4 pad_maximum_fusion
  221.0 0.4 fusion.17
  221.6 0.2 copy-done.3
  221.8 0.1 reshape.149
  222.1 0.6 gather_fusion.3
  222.7 0.6 gather_fusion.4
  223.4 0.7 select_bitcast_fusion
  224.1 0.2 fusion.23
  224.3 0.2 copy.155
  224.5 0.1 fusion.27
  224.6 0.1 copy.171
  224.7 0.8 fusion.10
  225.7 20.1 %all-gather.1 = f32[192,4,64]{2,1,0:T(4,128)S(1)} all-gather(f32[12,4,64]{2,1,0:T(4,128)S(1)} %copy.145), channel_id=3, replica_groups=mesh['group'=32,'tensor'=16] {'tensor'}, dimensions={0}, use_global_device_ids=true | all-gather | bytes 208896 | tf_op jit(solution)/shard_map/all_gather | solution.py:17
  245.9 21.4 %all-gather = f32[192,4,64]{2,1,0:T(4,128)S(1)} all-gather(f32[12,4,64]{2,1,0:T(4,128)S(1)} %pad_maximum_fusion.2), channel_id=2, replica_groups=mesh['group'=32,'tensor'=16] {'tensor'}, dimensions={0}, use_global_device_ids=true | all-gather | bytes 208896 | tf_op jit(solution)/shard_map/all_gather | solution.py:17
  267.3 124.1 %all-gather.5.cloned.1.call-done = f32[192,4,64,128]{3,2,1,0:T(8,128)} async-done(((f32[12,4,64,128]{3,2,1,0:T(8,128)}), f32[192,4,64,128]{3,2,1,0:T(8,128)}) %all-gather.5.cloned.1.call-update) | async-done | bytes 25165840 | tf_op jit(solution)/shard_map/all_gather | solution.py:17
  391.4 1.5 slice.56
  392.9 35.1 %while.19 = (s32[]{:T(128)}, f32[12,4,64]{2,1,0:T(4,128)S(1)}, f32[12,4,64]{2,1,0:T(4,128)S(1)}, f32[12,4,64,128]{3,2,1,0:T(8,128)S(1)}, f32[16,12,4,64]{3,2,1,0...) while((s32[]{:T(128)}, f32[12,4,64]{2,1,0:T(4,128)S(1)}, ...), condition=%wide.region_10.11_spmd, body=%wide.region_9.10_spmd.sunk | while | flops 1198085 | bytes 4841623 | solution.py:22
  393.0 2.3 fusion.49
  395.4 2.3 fusion.49
  397.7 2.3 fusion.49
  400.0 2.3 fusion.49
  402.4 2.3 fusion.49
  404.7 2.3 fusion.49
  407.1 2.3 fusion.49
  409.4 2.3 fusion.49
  411.7 2.3 fusion.49
  414.1 2.3 fusion.49
  416.4 2.3 fusion.49
  418.8 2.3 fusion.49
  421.1 2.3 fusion.49
  423.5 2.3 fusion.49
  425.8 2.3 fusion.49
  428.1 0.2 copy.151
  428.3 0.1 copy.158
  428.4 0.1 fusion.30
  428.5 0.7 copy.172
  429.3 0.9 copy.161
  430.2 1.0 copy.150
  431.2 0.2 copy.160
  431.5 0.8 multiply_add_fusion
  432.3 1.6 fusion.8
  (68 shorter events, 2.6 us)
Async XLA Ops:
  9.3 2.5 copy-start
  14.7 17.0 %copy-start.4 = (bf16[12,4,512]{2,1,0:T(4,128)(2,1)S(1)}, bf16[12,4,512]{2,1,0:T(4,128)(2,1)}, u32[]{:S(2)}) copy-start(bf16[12,4,512]{2,1,0:T(4,128)(2,1)} %param.12) | copy-start | bytes 147460
  14.7 200.2 %all-to-all-start = ((bf16[32,1,32,2048]{3,2,1,0:T(8,128)(2,1)}), bf16[32,1,32,2048]{3,2,1,0:T(8,128)(2,1)}, u32[]{:S(2)}, u32[]{:S(2)}) async-start(bf16[32,1,32,2048]{3,2,1,0:T(8,128)(2,1)} %bitcast.125), calls=%async_computation | async-start | bytes 8388608 | tf_op jit(solution)/shard_map/all_to_all | solution.py:123
  31.7 359.8 %all-gather.5.cloned.1.call-start = ((), (), s32[]{:S(2)}) async-start(), calls=%async_computation.1 | async-start | bytes 26738688 | tf_op jit(solution)/shard_map/all_gather | solution.py:17
  54.5 5.6 %copy-start.1 = (bf16[4,32,2048]{2,1,0:T(8,128)(2,1)S(1)}, bf16[4,32,2048]{2,1,0:T(8,128)(2,1)}, u32[]{:S(2)}) copy-start(bf16[4,32,2048]{2,1,0:T(8,128)(2,1)} %param.14) | copy-start | bytes 1572868
  58.6 1.6 copy-start.5
  220.9 0.9 copy-start.3
  428.3 1.9 copy-start.2
Sparse Core Ops, SparseCore 0:
  221.1 170.3 all-gather.4
where the time goes:
time: 442 us; the launch traced here: 441 us
  waiting for transfers between devices  278 us (63%)
  blocking collectives  64.1 us (15%)
  other arithmetic  40.4 us (9%)
  local copies, waits for them, and re-layouts  23.7 us (5%)
  starting transfers between devices  17 us (4%)
  between operations  13.8 us (3%)
    all_to_all x1, waiting for transfers between devices, body(): lax.all_to_all(outgoing.reshape(groups, per_pair, stride, features), 'gro...  153 us
    all_gather x1, waiting for transfers between devices, combined_all(): gathered = jax.tree.map(lambda a: lax.all_gather(a, axis), part)  124 us
    all_gather x2, blocking collectives, combined_all(): gathered = jax.tree.map(lambda a: lax.all_gather(a, axis), part)  41.5 us
    add x15, other arithmetic, combine(): earlier[2] * first_factor[..., None] + later[2] * second_factor[..., None]  34 us
    all_gather x1, blocking collectives, body(): asking = lax.all_gather(queries, 'tensor', axis=2, tiled=True)  22.6 us
    all_to_all x1, starting transfers between devices, body(): lax.all_to_all(outgoing.reshape(groups, per_pair, stride, features), 'gro...  16.9 us
  transfers between devices with their start and end apart: 2, of which 2 were waited for; matrix products, arithmetic and copies ran while one was open for 3% of the time, Pallas kernels for 0%

commit v1 on v0

--- a/solution.py
+++ b/solution.py
@@ -113,7 +113,16 @@
     arriving_rows = arriving // MIG_DEV * per_pair + ranking[arriving]
     arriving_kept = kept_by_slot[arriving]
     resident_len = lax.dynamic_slice_in_dim(resident_kept, group_here * RES_DEV, RES_DEV)
-    asking = lax.all_gather(queries, "tensor", axis=2, tiled=True)
+    ways = lax.axis_size("tensor")
+    up = [(d, (d + 1) % ways) for d in range(ways)]
+    down = [(d, (d - 1) % ways) for d in range(ways)]
+    earlier_2, later_2 = ([queries], [queries])
+    for _ in range(ways // 2):
+        earlier_2.append(lax.ppermute(earlier_2[-1], "tensor", up))
+    for _ in range((ways - 1) // 2):
+        later_2.append(lax.ppermute(later_2[-1], "tensor", down))
+    line = jnp.concatenate([*earlier_2[::-1], *later_2[1:]], axis=2)
+    asking = jnp.roll(line, (lax.axis_index("tensor") - ways // 2) * queries.shape[2], axis=2)
     resident_parts = partials(asking[:RES_DEV], resident_cache, resident_len, offset)
     outgoing = (
         jnp.zeros((groups * per_pair, stride, features), jnp.bfloat16)

time: 442 us -> 442 us (level)
  starting transfers between devices: 17 us -> 79.3 us
  waiting for transfers between devices: 278 us -> 234 us
  blocking collectives: 64.1 us -> 41.2 us
    ppermute x0 -> x15, starting transfers between devices: none -> 62.3 us  [the longest x7 45.7 us: body(): later_2.append(lax.ppermute(later_2[-1], 'tensor', down))]
    all_to_all x1, waiting for transfers between devices: 153 us -> 103 us  [body(): lax.all_to_all(outgoing.reshape(groups, per_pair, stride, features), 'gro...]
    all_gather x1 -> x0, blocking collectives: 22.6 us -> none  [body(): asking = lax.all_gather(queries, 'tensor', axis=2, tiled=True)]
    ppermute x0 -> x15, waiting for transfers between devices: none -> 7.25 us  [the longest x8 6.56 us: body(): earlier_2.append(lax.ppermute(earlier_2[-1], 'tensor', up))]
  transfers between devices with their start and end apart: 2 -> 17, of which waited for: 2 -> 4; matrix products, arithmetic and copies ran while one was open for 3% -> 3% of each run, Pallas kernels for 0% -> 0%
where the time goes in v1:
time: 442 us; the launch traced here: 441 us
  waiting for transfers between devices  234 us (53%)
  starting transfers between devices  79.3 us (18%)
  blocking collectives  41.2 us (9%)
  other arithmetic  40.4 us (9%)
  local copies, waits for them, and re-layouts  27.3 us (6%)
  between operations  14.2 us (3%)
    all_gather x1, waiting for transfers between devices, combined_all(): gathered = jax.tree.map(lambda a: lax.all_gather(a, axis), part)  124 us
    all_to_all x1, waiting for transfers between devices, body(): lax.all_to_all(outgoing.reshape(groups, per_pair, stride, features), 'gro...  103 us
    ppermute x7, starting transfers between devices, body(): later_2.append(lax.ppermute(later_2[-1], 'tensor', down))  45.7 us
    all_gather x2, blocking collectives, combined_all(): gathered = jax.tree.map(lambda a: lax.all_gather(a, axis), part)  41.2 us
    add x15, other arithmetic, combine(): earlier[2] * first_factor[..., None] + later[2] * second_factor[..., None]  34 us
    all_to_all x1, starting transfers between devices, body(): lax.all_to_all(outgoing.reshape(groups, per_pair, stride, features), 'gro...  17 us
    ppermute x8, starting transfers between devices, body(): earlier_2.append(lax.ppermute(earlier_2[-1], 'tensor', up))  16.6 us
  transfers between devices with their start and end apart: 17, of which 4 were waited for; matrix products, arithmetic and copies ran while one was open for 3% of the time, Pallas kernels for 0%

profile of v1, /device:TPU:1, one launch (start us, length us, event | category | flops | bytes accessed | tf_op | source)
XLA Modules:
  0.0 440.8 jit_solution(11011536320553174350)
XLA Ops:
  6.5 0.7 compare_select_fusion
  7.2 1.6 scatter_custom_fusion.2
  9.3 2.5 broadcast_in_dim.118
  11.8 2.9 scatter_fusion
  14.7 17.0 %all-to-all-start = ((bf16[32,1,32,2048]{3,2,1,0:T(8,128)(2,1)}), bf16[32,1,32,2048]{3,2,1,0:T(8,128)(2,1)}, u32[]{:S(2)}, u32[]{:S(2)}) async-start(bf16[32,1,32,2048]{3,2,1,0:T(8,128)(2,1)} %bitcast.125), calls=%async_computation | async-start | bytes 8388608 | tf_op jit(solution)/shard_map/all_to_all | solution.py:132
  31.8 3.1 collective-permute-start
  34.9 5.6 %collective-permute-start.8 = (bf16[12,4,512]{2,1,0:T(4,128)(2,1)S(1)}, bf16[12,4,512]{2,1,0:T(4,128)(2,1)S(1)}, u32[]{:S(2)}, u32[]{:S(2)}) collective-permute-start(bf16[12,4,512]{2,1,0:T(4,128)(2,1)S(1)} %copy-done.3), channel_id=1, source_target_pairs={{0,15},{1,0},{2,1},{3,2},{4,3},{5,4},{6,5},{7,6},{8,7},{9,8},{10,9... | collective-permute-start | bytes 147464 | tf_op jit(solution)/shard_map/ppermute | solution.py:123
  40.8 1.6 scatter_custom_fusion.1
  42.4 1.9 collective-permute-start.1
  44.4 6.5 %collective-permute-done.1 = bf16[12,4,512]{2,1,0:T(4,128)(2,1)S(1)} collective-permute-done((bf16[12,4,512]{2,1,0:T(4,128)(2,1)S(1)}, bf16[12,4,512]{2,1,0:T(4,128)(2,1)S(1)}, u32[]{:S(2)}, u32[]{:S(2)}) %collective-permute-start.1) | collective-permute-done | bytes 49184 | tf_op jit(solution)/shard_map/ppermute | solution.py:121
  50.9 1.9 collective-permute-start.2
  52.9 6.7 %collective-permute-start.9 = (bf16[12,4,512]{2,1,0:T(4,128)(2,1)S(1)}, bf16[12,4,512]{2,1,0:T(4,128)(2,1)S(1)}, u32[]{:S(2)}, u32[]{:S(2)}) collective-permute-start(bf16[12,4,512]{2,1,0:T(4,128)(2,1)S(1)} %collective-permute-done.8), channel_id=1, source_target_pairs={{0,15},{1,0},{2,1},{3,2},{4,3},{5,4},{6,5},{7,6},{8,7},{9,8},{10,9... | collective-permute-start | bytes 147464 | tf_op jit(solution)/shard_map/ppermute | solution.py:123
  59.6 1.9 collective-permute-start.3
  61.5 1.6 scatter_custom_fusion
  63.1 0.6 gather_fusion
  63.7 6.7 %collective-permute-start.10 = (bf16[12,4,512]{2,1,0:T(4,128)(2,1)S(1)}, bf16[12,4,512]{2,1,0:T(4,128)(2,1)S(1)}, u32[]{:S(2)}, u32[]{:S(2)}) collective-permute-start(bf16[12,4,512]{2,1,0:T(4,128)(2,1)S(1)} %collective-permute-done.9), channel_id=1, source_target_pairs={{0,15},{1,0},{2,1},{3,2},{4,3},{5,4},{6,5},{7,6},{8,7},{9,8},{10,9... | collective-permute-start | bytes 147464 | tf_op jit(solution)/shard_map/ppermute | solution.py:123
  70.4 1.9 collective-permute-start.4
  72.5 6.7 %collective-permute-start.11 = (bf16[12,4,512]{2,1,0:T(4,128)(2,1)S(1)}, bf16[12,4,512]{2,1,0:T(4,128)(2,1)S(1)}, u32[]{:S(2)}, u32[]{:S(2)}) collective-permute-start(bf16[12,4,512]{2,1,0:T(4,128)(2,1)S(1)} %collective-permute-done.10), channel_id=1, source_target_pairs={{0,15},{1,0},{2,1},{3,2},{4,3},{5,4},{6,5},{7,6},{8,7},{9,8},{10,9... | collective-permute-start | bytes 147464 | tf_op jit(solution)/shard_map/ppermute | solution.py:123
  79.2 1.9 collective-permute-start.5
  81.2 0.6 gather_fusion.1
  81.8 6.7 %collective-permute-start.12 = (bf16[12,4,512]{2,1,0:T(4,128)(2,1)S(1)}, bf16[12,4,512]{2,1,0:T(4,128)(2,1)S(1)}, u32[]{:S(2)}, u32[]{:S(2)}) collective-permute-start(bf16[12,4,512]{2,1,0:T(4,128)(2,1)S(1)} %collective-permute-done.11), channel_id=1, source_target_pairs={{0,15},{1,0},{2,1},{3,2},{4,3},{5,4},{6,5},{7,6},{8,7},{9,8},{10,9... | collective-permute-start | bytes 147464 | tf_op jit(solution)/shard_map/ppermute | solution.py:123
  88.5 1.9 collective-permute-start.6
  90.6 6.7 %collective-permute-start.13 = (bf16[12,4,512]{2,1,0:T(4,128)(2,1)S(1)}, bf16[12,4,512]{2,1,0:T(4,128)(2,1)S(1)}, u32[]{:S(2)}, u32[]{:S(2)}) collective-permute-start(bf16[12,4,512]{2,1,0:T(4,128)(2,1)S(1)} %collective-permute-done.12), channel_id=1, source_target_pairs={{0,15},{1,0},{2,1},{3,2},{4,3},{5,4},{6,5},{7,6},{8,7},{9,8},{10,9... | collective-permute-start | bytes 147464 | tf_op jit(solution)/shard_map/ppermute | solution.py:123
  97.3 1.9 collective-permute-start.7
  99.2 6.7 %collective-permute-start.14 = (bf16[12,4,512]{2,1,0:T(4,128)(2,1)S(1)}, bf16[12,4,512]{2,1,0:T(4,128)(2,1)S(1)}, u32[]{:S(2)}, u32[]{:S(2)}) collective-permute-start(bf16[12,4,512]{2,1,0:T(4,128)(2,1)S(1)} %collective-permute-done.13), channel_id=1, source_target_pairs={{0,15},{1,0},{2,1},{3,2},{4,3},{5,4},{6,5},{7,6},{8,7},{9,8},{10,9... | collective-permute-start | bytes 147464 | tf_op jit(solution)/shard_map/ppermute | solution.py:123
  106.4 0.7 collective-permute-done.14
  107.6 1.2 copy-done.2
  110.0 1.2 constant_dynamic-slice_fusion.1
  111.2 0.5 reshape.250
  111.7 103.2 %all-to-all-done = bf16[32,1,32,2048]{3,2,1,0:T(8,128)(2,1)} async-done(((bf16[32,1,32,2048]{3,2,1,0:T(8,128)(2,1)}), bf16[32,1,32,2048]{3,2,1,0:T(8,128)(2,1)}, u32[]{:S(2)}, u32[]{:S(2)}) %all-to-all-start) | async-done | bytes 4194336 | tf_op jit(solution)/shard_map/all_to_all | solution.py:132
  215.0 2.8 gather_fusion.2
  218.2 0.5 select_reduce_fusion
  218.7 0.7 convolution_bitcast_fusion
  219.6 1.4 pad_maximum_fusion
  220.9 0.9 copy-done.5
  222.1 0.6 gather_fusion.3
  222.7 0.6 gather_fusion.4
  223.4 0.7 select_bitcast_fusion
  225.4 0.8 fusion.10
  226.3 20.7 %all-gather.1 = f32[192,4,64]{2,1,0:T(4,128)S(1)} all-gather(f32[12,4,64]{2,1,0:T(4,128)S(1)} %copy.145), channel_id=3, replica_groups=mesh['group'=32,'tensor'=16] {'tensor'}, dimensions={0}, use_global_device_ids=true | all-gather | bytes 208896 | tf_op jit(solution)/shard_map/all_gather | solution.py:17
  247.1 20.5 %all-gather = f32[192,4,64]{2,1,0:T(4,128)S(1)} all-gather(f32[12,4,64]{2,1,0:T(4,128)S(1)} %pad_maximum_fusion.2), channel_id=2, replica_groups=mesh['group'=32,'tensor'=16] {'tensor'}, dimensions={0}, use_global_device_ids=true | all-gather | bytes 208896 | tf_op jit(solution)/shard_map/all_gather | solution.py:17
  267.7 123.8 %all-gather.5.cloned.1.call-done = f32[192,4,64,128]{3,2,1,0:T(8,128)} async-done(((f32[12,4,64,128]{3,2,1,0:T(8,128)}), f32[192,4,64,128]{3,2,1,0:T(8,128)}) %all-gather.5.cloned.1.call-update) | async-done | bytes 25165840 | tf_op jit(solution)/shard_map/all_gather | solution.py:17
  391.4 1.5 slice.54
  392.9 35.1 %while.19 = (s32[]{:T(128)}, f32[12,4,64]{2,1,0:T(4,128)S(1)}, f32[12,4,64]{2,1,0:T(4,128)S(1)}, f32[12,4,64,128]{3,2,1,0:T(8,128)S(1)}, f32[16,12,4,64]{3,2,1,0...) while((s32[]{:T(128)}, f32[12,4,64]{2,1,0:T(4,128)S(1)}, ...), condition=%wide.region_10.11_spmd, body=%wide.region_9.10_spmd.sunk | while | flops 1198085 | bytes 4841623 | solution.py:22
  393.0 2.3 fusion.49
  395.4 2.3 fusion.49
  397.7 2.3 fusion.49
  400.0 2.3 fusion.49
  402.4 2.3 fusion.49
  404.7 2.3 fusion.49
  407.1 2.3 fusion.49
  409.4 2.3 fusion.49
  411.7 2.3 fusion.49
  414.1 2.3 fusion.49
  416.4 2.3 fusion.49
  418.8 2.3 fusion.49
  421.1 2.3 fusion.49
  423.5 2.3 fusion.49
  425.8 2.3 fusion.49
  428.5 0.7 copy.172
  429.3 1.0 copy.161
  430.2 1.0 copy.150
  431.5 0.8 multiply_add_fusion
  432.3 1.6 fusion.8
  (131 shorter events, 6.9 us)
Async XLA Ops:
  9.3 2.5 copy-start
  14.7 17.0 %copy-start.3 = (bf16[12,4,512]{2,1,0:T(4,128)(2,1)S(1)}, bf16[12,4,512]{2,1,0:T(4,128)(2,1)}, u32[]{:S(2)}) copy-start(bf16[12,4,512]{2,1,0:T(4,128)(2,1)} %param.12) | copy-start | bytes 147460
  14.7 25.8 %copy-start.1 = (bf16[4,32,2048]{2,1,0:T(8,128)(2,1)S(1)}, bf16[4,32,2048]{2,1,0:T(8,128)(2,1)}, u32[]{:S(2)}) copy-start(bf16[4,32,2048]{2,1,0:T(8,128)(2,1)} %param.14) | copy-start | bytes 1572868
  14.7 200.2 %all-to-all-start = ((bf16[32,1,32,2048]{3,2,1,0:T(8,128)(2,1)}), bf16[32,1,32,2048]{3,2,1,0:T(8,128)(2,1)}, u32[]{:S(2)}, u32[]{:S(2)}) async-start(bf16[32,1,32,2048]{3,2,1,0:T(8,128)(2,1)} %bitcast.125), calls=%async_computation | async-start | bytes 8388608 | tf_op jit(solution)/shard_map/all_to_all | solution.py:132
  31.7 40.7 %copy-start.6 = (s32[128]{0:T(128)S(1)}, s32[128]{0:T(128)}, u32[]{:S(2)}) copy-start(s32[128]{0:T(128)} %param.16) | copy-start | bytes 1540
  31.7 359.7 %all-gather.5.cloned.1.call-start = ((), (), s32[]{:S(2)}) async-start(), calls=%async_computation.1 | async-start | bytes 26738688 | tf_op jit(solution)/shard_map/all_gather | solution.py:17
  31.8 10.6 %collective-permute-start = (bf16[12,4,512]{2,1,0:T(4,128)(2,1)S(1)}, bf16[12,4,512]{2,1,0:T(4,128)(2,1)S(1)}, u32[]{:S(2)}, u32[]{:S(2)}) collective-permute-start(bf16[12,4,512]{2,1,0:T(4,128)(2,1)S(1)} %copy-done.3), channel_id=1, source_target_pairs={{0,1},{1,2},{2,3},{3,4},{4,5},{5,6},{6,7},{7,8},{8,9},{9,10},{10,1... | collective-permute-start | bytes 147464 | tf_op jit(solution)/shard_map/ppermute | solution.py:121
  34.9 17.9 %collective-permute-start.8 = (bf16[12,4,512]{2,1,0:T(4,128)(2,1)S(1)}, bf16[12,4,512]{2,1,0:T(4,128)(2,1)S(1)}, u32[]{:S(2)}, u32[]{:S(2)}) collective-permute-start(bf16[12,4,512]{2,1,0:T(4,128)(2,1)S(1)} %copy-done.3), channel_id=1, source_target_pairs={{0,15},{1,0},{2,1},{3,2},{4,3},{5,4},{6,5},{7,6},{8,7},{9,8},{10,9... | collective-permute-start | bytes 147464 | tf_op jit(solution)/shard_map/ppermute | solution.py:123
  42.4 8.6 %collective-permute-start.1 = (bf16[12,4,512]{2,1,0:T(4,128)(2,1)S(1)}, bf16[12,4,512]{2,1,0:T(4,128)(2,1)S(1)}, u32[]{:S(2)}, u32[]{:S(2)}) collective-permute-start(bf16[12,4,512]{2,1,0:T(4,128)(2,1)S(1)} %collective-permute-done), channel_id=1, source_target_pairs={{0,1},{1,2},{2,3},{3,4},{4,5},{5,6},{6,7},{7,8},{8,9},{9,10},{10,1... | collective-permute-start | bytes 147464 | tf_op jit(solution)/shard_map/ppermute | solution.py:121
  50.9 8.6 %collective-permute-start.2 = (bf16[12,4,512]{2,1,0:T(4,128)(2,1)S(1)}, bf16[12,4,512]{2,1,0:T(4,128)(2,1)S(1)}, u32[]{:S(2)}, u32[]{:S(2)}) collective-permute-start(bf16[12,4,512]{2,1,0:T(4,128)(2,1)S(1)} %collective-permute-done.1), channel_id=1, source_target_pairs={{0,1},{1,2},{2,3},{3,4},{4,5},{5,6},{6,7},{7,8},{8,9},{9,10},{10,1... | collective-permute-start | bytes 147464 | tf_op jit(solution)/shard_map/ppermute | solution.py:121
  52.9 10.8 %collective-permute-start.9 = (bf16[12,4,512]{2,1,0:T(4,128)(2,1)S(1)}, bf16[12,4,512]{2,1,0:T(4,128)(2,1)S(1)}, u32[]{:S(2)}, u32[]{:S(2)}) collective-permute-start(bf16[12,4,512]{2,1,0:T(4,128)(2,1)S(1)} %collective-permute-done.8), channel_id=1, source_target_pairs={{0,15},{1,0},{2,1},{3,2},{4,3},{5,4},{6,5},{7,6},{8,7},{9,8},{10,9... | collective-permute-start | bytes 147464 | tf_op jit(solution)/shard_map/ppermute | solution.py:123
  59.6 10.8 %collective-permute-start.3 = (bf16[12,4,512]{2,1,0:T(4,128)(2,1)S(1)}, bf16[12,4,512]{2,1,0:T(4,128)(2,1)S(1)}, u32[]{:S(2)}, u32[]{:S(2)}) collective-permute-start(bf16[12,4,512]{2,1,0:T(4,128)(2,1)S(1)} %collective-permute-done.2), channel_id=1, source_target_pairs={{0,1},{1,2},{2,3},{3,4},{4,5},{5,6},{6,7},{7,8},{8,9},{9,10},{10,1... | collective-permute-start | bytes 147464 | tf_op jit(solution)/shard_map/ppermute | solution.py:121
  63.7 8.8 %collective-permute-start.10 = (bf16[12,4,512]{2,1,0:T(4,128)(2,1)S(1)}, bf16[12,4,512]{2,1,0:T(4,128)(2,1)S(1)}, u32[]{:S(2)}, u32[]{:S(2)}) collective-permute-start(bf16[12,4,512]{2,1,0:T(4,128)(2,1)S(1)} %collective-permute-done.9), channel_id=1, source_target_pairs={{0,15},{1,0},{2,1},{3,2},{4,3},{5,4},{6,5},{7,6},{8,7},{9,8},{10,9... | collective-permute-start | bytes 147464 | tf_op jit(solution)/shard_map/ppermute | solution.py:123
  70.4 8.8 %collective-permute-start.4 = (bf16[12,4,512]{2,1,0:T(4,128)(2,1)S(1)}, bf16[12,4,512]{2,1,0:T(4,128)(2,1)S(1)}, u32[]{:S(2)}, u32[]{:S(2)}) collective-permute-start(bf16[12,4,512]{2,1,0:T(4,128)(2,1)S(1)} %collective-permute-done.3), channel_id=1, source_target_pairs={{0,1},{1,2},{2,3},{3,4},{4,5},{5,6},{6,7},{7,8},{8,9},{9,10},{10,1... | collective-permute-start | bytes 147464 | tf_op jit(solution)/shard_map/ppermute | solution.py:121
  72.5 9.3 %collective-permute-start.11 = (bf16[12,4,512]{2,1,0:T(4,128)(2,1)S(1)}, bf16[12,4,512]{2,1,0:T(4,128)(2,1)S(1)}, u32[]{:S(2)}, u32[]{:S(2)}) collective-permute-start(bf16[12,4,512]{2,1,0:T(4,128)(2,1)S(1)} %collective-permute-done.10), channel_id=1, source_target_pairs={{0,15},{1,0},{2,1},{3,2},{4,3},{5,4},{6,5},{7,6},{8,7},{9,8},{10,9... | collective-permute-start | bytes 147464 | tf_op jit(solution)/shard_map/ppermute | solution.py:123
  79.2 9.3 %collective-permute-start.5 = (bf16[12,4,512]{2,1,0:T(4,128)(2,1)S(1)}, bf16[12,4,512]{2,1,0:T(4,128)(2,1)S(1)}, u32[]{:S(2)}, u32[]{:S(2)}) collective-permute-start(bf16[12,4,512]{2,1,0:T(4,128)(2,1)S(1)} %collective-permute-done.4), channel_id=1, source_target_pairs={{0,1},{1,2},{2,3},{3,4},{4,5},{5,6},{6,7},{7,8},{8,9},{9,10},{10,1... | collective-permute-start | bytes 147464 | tf_op jit(solution)/shard_map/ppermute | solution.py:121
  81.8 8.7 %collective-permute-start.12 = (bf16[12,4,512]{2,1,0:T(4,128)(2,1)S(1)}, bf16[12,4,512]{2,1,0:T(4,128)(2,1)S(1)}, u32[]{:S(2)}, u32[]{:S(2)}) collective-permute-start(bf16[12,4,512]{2,1,0:T(4,128)(2,1)S(1)} %collective-permute-done.11), channel_id=1, source_target_pairs={{0,15},{1,0},{2,1},{3,2},{4,3},{5,4},{6,5},{7,6},{8,7},{9,8},{10,9... | collective-permute-start | bytes 147464 | tf_op jit(solution)/shard_map/ppermute | solution.py:123
  88.5 8.7 %collective-permute-start.6 = (bf16[12,4,512]{2,1,0:T(4,128)(2,1)S(1)}, bf16[12,4,512]{2,1,0:T(4,128)(2,1)S(1)}, u32[]{:S(2)}, u32[]{:S(2)}) collective-permute-start(bf16[12,4,512]{2,1,0:T(4,128)(2,1)S(1)} %collective-permute-done.5), channel_id=1, source_target_pairs={{0,1},{1,2},{2,3},{3,4},{4,5},{5,6},{6,7},{7,8},{8,9},{9,10},{10,1... | collective-permute-start | bytes 147464 | tf_op jit(solution)/shard_map/ppermute | solution.py:121
  90.6 8.7 %collective-permute-start.13 = (bf16[12,4,512]{2,1,0:T(4,128)(2,1)S(1)}, bf16[12,4,512]{2,1,0:T(4,128)(2,1)S(1)}, u32[]{:S(2)}, u32[]{:S(2)}) collective-permute-start(bf16[12,4,512]{2,1,0:T(4,128)(2,1)S(1)} %collective-permute-done.12), channel_id=1, source_target_pairs={{0,15},{1,0},{2,1},{3,2},{4,3},{5,4},{6,5},{7,6},{8,7},{9,8},{10,9... | collective-permute-start | bytes 147464 | tf_op jit(solution)/shard_map/ppermute | solution.py:123
  97.3 8.7 %collective-permute-start.7 = (bf16[12,4,512]{2,1,0:T(4,128)(2,1)S(1)}, bf16[12,4,512]{2,1,0:T(4,128)(2,1)S(1)}, u32[]{:S(2)}, u32[]{:S(2)}) collective-permute-start(bf16[12,4,512]{2,1,0:T(4,128)(2,1)S(1)} %collective-permute-done.6), channel_id=1, source_target_pairs={{0,1},{1,2},{2,3},{3,4},{4,5},{5,6},{6,7},{7,8},{8,9},{9,10},{10,1... | collective-permute-start | bytes 147464 | tf_op jit(solution)/shard_map/ppermute | solution.py:121
  99.2 7.8 %collective-permute-start.14 = (bf16[12,4,512]{2,1,0:T(4,128)(2,1)S(1)}, bf16[12,4,512]{2,1,0:T(4,128)(2,1)S(1)}, u32[]{:S(2)}, u32[]{:S(2)}) collective-permute-start(bf16[12,4,512]{2,1,0:T(4,128)(2,1)S(1)} %collective-permute-done.13), channel_id=1, source_target_pairs={{0,15},{1,0},{2,1},{3,2},{4,3},{5,4},{6,5},{7,6},{8,7},{9,8},{10,9... | collective-permute-start | bytes 147464 | tf_op jit(solution)/shard_map/ppermute | solution.py:123
  107.6 1.2 copy-start.2
  220.9 0.9 copy-start.5
  428.3 1.9 copy-start.4
Sparse Core Ops, SparseCore 0:
  221.1 170.3 all-gather.4
